TPU v7x, 1024 devices: a whole 4x4x32 slice. The times are simulated.
1024 devices in a mesh: dp: 32 (over y, z_lo), rows: 32 (over z_hi, x, core).
Axes of the slice: x: 4, y: 4, z: 32 (z_hi: 4, z_lo: 8; z = z_hi * 8 + z_lo), core: 2. Of those that a mesh axis runs over, the one named last changes fastest.
Arguments:
- images: bfloat16 [32, 256, 64, 384], P('dp', 'rows'), may hold values from -6 to 6
- kernel: float32 [7, 7, 384], replicated, may hold values from -0.875 to 0.875
- conv_bias: float32 [384], replicated, may hold values from -3 to 3
- norm_gain: float32 [384], replicated, may hold values from 0.5 to 1.5
- norm_shift: float32 [384], replicated, may hold values from -3 to 3
- up_weight: bfloat16 [384, 1536], replicated, may hold values from -0.3125 to 0.3125
- up_bias: float32 [1536], replicated, may hold values from -3 to 3
- down_weight: bfloat16 [384, 1536], replicated, may hold values from -0.15625 to 0.15625
- layer_scale: float32 [384], replicated, may hold values from 0.5 to 1.5
- cotangent: bfloat16 [32, 256, 64, 384], P('dp', 'rows'), may hold values from -6 to 6
Outputs:
- grad_images: bfloat16 [32, 256, 64, 384], P('dp', 'rows')
- grad_up: float32 [384, 1536], P('dp', 'rows')
- grad_down: float32 [384, 1536], P('dp', 'rows')
All inputs are finite; a program needn't handle non-finite values.
Results may differ from a plain program's by a relative error of at most 0.023.
Values may be sent and summed in bfloat16 or wider, within the bound.
A program may use at most 128 MiB of HBM per device.

v0:
```python
import math

import jax
import jax.numpy as jnp
from jax import lax
from jax.sharding import PartitionSpec as P

EPSILON = 1e-06


def extended_2(cells, sides, width):
    for axis, dim in sides:
        count = lax.axis_size(axis)
        ends = count - 1
        head = lax.slice_in_dim(cells, 0, width, axis=dim)
        tail = lax.slice_in_dim(cells, cells.shape[dim] - width, cells.shape[dim], axis=dim)
        cells = jnp.concatenate(
            [
                lax.ppermute(tail, axis, [(i, (i + 1) % count) for i in range(ends)]),
                cells,
                lax.ppermute(head, axis, [((i + 1) % count, i) for i in range(ends)]),
            ],
            axis=dim,
        )
    return cells


def depthwise(padded, kernel):
    return lax.conv_general_dilated(
        padded,
        kernel[:, :, None, :],
        (1, 1),
        "VALID",
        dimension_numbers=("NHWC", "HWIO", "NHWC"),
        feature_group_count=kernel.shape[2],
        precision=lax.Precision.HIGHEST,
    )


def gelu_slope(values):
    normal_cdf = 0.5 * (1.0 + jax.scipy.special.erf(values * (1.0 / math.sqrt(2.0))))
    density = jnp.exp(-0.5 * values * values) * (1.0 / math.sqrt(2.0 * math.pi))
    return normal_cdf + values * density


def block_terms(
    conv_out, norm_gain, norm_shift, up_weight, up_bias, down_weight, layer_scale, cotangent
):
    row_mean = jnp.mean(conv_out, axis=1, keepdims=True)
    centered = conv_out - row_mean
    inverse = lax.rsqrt(jnp.mean(centered * centered, axis=1, keepdims=True) + EPSILON)
    standard = centered * inverse
    normed = (standard * norm_gain + norm_shift).astype(jnp.bfloat16)
    before = jnp.dot(normed, up_weight, preferred_element_type=jnp.float32) + up_bias
    activated = jax.nn.gelu(before, approximate=False).astype(jnp.bfloat16)
    scaled = (cotangent.astype(jnp.float32) * layer_scale).astype(jnp.bfloat16)
    grad_act = jnp.dot(scaled, down_weight, preferred_element_type=jnp.float32)
    term_down = lax.dot_general(
        scaled, activated, (((0,), (0,)), ((), ())), preferred_element_type=jnp.float32
    )
    grad_before = (grad_act * gelu_slope(before)).astype(jnp.bfloat16)
    term_up = lax.dot_general(
        normed, grad_before, (((0,), (0,)), ((), ())), preferred_element_type=jnp.float32
    )
    grad_normed = lax.dot_general(
        grad_before, up_weight, (((1,), (1,)), ((), ())), preferred_element_type=jnp.float32
    )
    gscaled = grad_normed * norm_gain
    grad_conv = inverse * (
        gscaled
        - jnp.mean(gscaled, axis=1, keepdims=True)
        - standard * jnp.mean(gscaled * standard, axis=1, keepdims=True)
    )
    return (grad_conv.astype(jnp.bfloat16), term_up, term_down)


def on_device(
    images,
    kernel,
    conv_bias,
    norm_gain,
    norm_shift,
    up_weight,
    up_bias,
    down_weight,
    layer_scale,
    cotangent,
):
    reach = kernel.shape[0] // 2
    shape = images.shape
    channels = shape[3]
    side_pad = ((0, 0), (0, 0), (reach, reach), (0, 0))
    extended = extended_2(images, (("rows", 1),), reach)
    padded = jnp.pad(extended.astype(jnp.float32), side_pad)
    conv_out = depthwise(padded, kernel) + conv_bias
    grad_conv, term_up, term_down = block_terms(
        conv_out.reshape(-1, channels),
        norm_gain,
        norm_shift,
        up_weight,
        up_bias,
        down_weight,
        layer_scale,
        cotangent.reshape(-1, channels),
    )
    grad_ext = extended_2(grad_conv.reshape(shape), (("rows", 1),), reach)
    grad_pad = jnp.pad(grad_ext.astype(jnp.float32), side_pad)
    back = depthwise(grad_pad, kernel[::-1, ::-1])
    grad_images = (cotangent.astype(jnp.float32) + back).astype(jnp.bfloat16)
    groups = lax.axis_size("dp")
    parts = lax.axis_size("rows")
    factor = 1.0 / math.sqrt(shape[0] * shape[1] * shape[2] * groups * parts)
    term_up = term_up * factor
    term_down = term_down * factor
    halves = (
        lax.psum_scatter(
            term_up.astype(jnp.bfloat16), "rows", scatter_dimension=1, tiled=True
        ).astype(jnp.float32),
        lax.psum_scatter(
            term_down.astype(jnp.bfloat16), "rows", scatter_dimension=1, tiled=True
        ).astype(jnp.float32),
    )
    grad_up, grad_down = (
        lax.psum_scatter(halves[0], "dp", scatter_dimension=0, tiled=True),
        lax.psum_scatter(halves[1], "dp", scatter_dimension=0, tiled=True),
    )
    return (grad_images, grad_up, grad_down)


def solution(mesh):
    in_specs = (
        P("dp", "rows", None, None),
        P(),
        P(),
        P(),
        P(),
        P(),
        P(),
        P(),
        P(),
        P("dp", "rows", None, None),
    )
    out_specs = (P("dp", "rows", None, None), P("dp", "rows"), P("dp", "rows"))
    return jax.shard_map(
        on_device, mesh=mesh, in_specs=in_specs, out_specs=out_specs, check_vma=False
    )
```

profile of v0, /device:TPU:6, one launch (start us, length us, event | category | flops | bytes accessed | tf_op | source)
XLA Modules:
  0.0 642.6 jit_solution(10378891809642843489)
XLA Ops:
  7.2 1.1 fusion.91
  8.3 1.9 collective-permute-start
  10.3 3.6 collective-permute-start.1
  13.9 1.1 fusion.46
  15.0 11.8 %collective-permute-done.1 = bf16[1,3,64,384]{3,2,1,0:T(8,128)(2,1)S(1)} collective-permute-done((bf16[1,3,64,384]{3,2,1,0:T(8,128)(2,1)S(1)}, bf16[1,3,64,384]{3,2,1,0:T(8,128)(2,1)S(1)}, u32[]{:S(2)}, u32[]{:S(2)}) %collective-permute-start.1) | collective-permute-done | bytes 147488 | tf_op jit(solution)/shard_map/ppermute | solution.py:21
  26.9 1.1 maximum_bitcast_fusion.1
  28.9 3.2 fusion.40
  33.5 1.0 convolution_add_fusion
  34.8 2.5 fusion.14
  37.3 3.5 fusion.15
  40.8 2.5 fusion.89
  43.6 9.4 %fusion.16 = bf16[384,1536]{0,1:T(8,128)(2,1)} fusion(bf16[512,384]{1,0:T(8,128)(2,1)S(1)} %fusion.46, f32[512,1536]{1,0:T(8,128)} %copy-done.9), kind=kOutput, calls=%fused_computation.30 | convolution fusion | flops 656277504 | bytes 4718592 | tf_op jit(solution)/shard_map/dot_general | solution.py:58
  53.8 21.2 %collective-permute-start.2 = (bf16[1,3,64,384]{3,1,2,0:T(4,128)(2,1)S(1)}, bf16[1,3,64,384]{3,1,2,0:T(4,128)(2,1)S(1)}, u32[]{:S(2)}, u32[]{:S(2)}) collective-permute-start(bf16[1,3,64,384]{3,1,2,0:T(4,128)(2,1)S(1)} %get-tuple-element.24), channel_id=1, source_target_pairs={{0,1},{1,2},{2,3},{3,4},{4,5},{5,6},{6,7},{7,8},{8,9},{9,10},{10,1... | collective-permute-start | bytes 442376 | tf_op jit(solution)/shard_map/ppermute | solution.py:19
  75.0 1.9 collective-permute-start.3
  77.0 1.3 dynamic-slice
  79.0 1.1 collective-permute-done.3
  80.9 3.1 fusion.34
  84.3 0.7 copy-done.1
  85.1 0.9 fusion.44
  86.0 148.0 %reduce-scatter.5.cloned.1.call-done = bf16[384,48]{0,1:T(8,128)(2,1)} async-done(((bf16[384,1536]{0,1:T(8,128)(2,1)}), bf16[384,48]{0,1:T(8,128)(2,1)}) %reduce-scatter.5.cloned.1.call-update) | async-done | bytes 36880 | tf_op jit(solution)/shard_map/reduce_scatter | solution.py:116
  234.0 163.6 %reduce-scatter.7.cloned.1.call-done = bf16[384,48]{0,1:T(8,128)(2,1)} async-done(((bf16[384,1536]{0,1:T(8,128)(2,1)}), bf16[384,48]{0,1:T(8,128)(2,1)}) %reduce-scatter.7.cloned.1.call-update) | async-done | bytes 36880 | tf_op jit(solution)/shard_map/reduce_scatter | solution.py:119
  397.6 236.7 %all-reduce.4 = (f32[384,48]{0,1:T(8,128)S(1)}, f32[384,48]{0,1:T(8,128)S(1)}) all-reduce(bf16[384,48]{0,1:T(8,128)(2,1)} %reduce-scatter.5.cloned.1.call-done, bf16[384,48]{0,1:T(8,128)(2,1)} %reduce-scatter.7.cloned.1.call-done), channel_id=3, replica_groups=mesh['dp'=32,'rows'=32] {'dp'}, use_global_device_ids=true, to_apply=%region_5.6.clone | all-reduce | flops 36864 | bytes 221184
  634.4 0.7 copy.86
  635.1 0.7 copy.87
  (53 shorter events, 4.8 us)
Async XLA Ops:
  7.2 26.3 %copy-start = (bf16[384,1536]{1,0:T(8,128)(2,1)S(1)}, bf16[384,1536]{1,0:T(8,128)(2,1)}, u32[]{:S(2)}) copy-start(bf16[384,1536]{1,0:T(8,128)(2,1)} %param.15) | copy-start | bytes 3538948
  7.2 226.8 %reduce-scatter.5.cloned.1.call-start = ((), (), s32[]{:S(2)}) async-start(), calls=%async_computation.2 | async-start | bytes 1216512 | tf_op jit(solution)/shard_map/reduce_scatter | solution.py:116
  8.3 6.7 %collective-permute-start = (bf16[1,3,64,384]{3,2,1,0:T(8,128)(2,1)S(1)}, bf16[1,3,64,384]{3,2,1,0:T(8,128)(2,1)S(1)}, u32[]{:S(2)}, u32[]{:S(2)}) collective-permute-start(bf16[1,3,64,384]{3,2,1,0:T(8,128)(2,1)S(1)} %get-tuple-element.26), channel_id=1, source_target_pairs={{0,1},{1,2},{2,3},{3,4},{4,5},{5,6},{6,7},{7,8},{8,9},{9,10},{10,1... | collective-permute-start | bytes 442376 | tf_op jit(solution)/shard_map/ppermute | solution.py:19
  10.3 16.6 %collective-permute-start.1 = (bf16[1,3,64,384]{3,2,1,0:T(8,128)(2,1)S(1)}, bf16[1,3,64,384]{3,2,1,0:T(8,128)(2,1)S(1)}, u32[]{:S(2)}, u32[]{:S(2)}) collective-permute-start(bf16[1,3,64,384]{3,2,1,0:T(8,128)(2,1)S(1)} %get-tuple-element.27), channel_id=1, source_target_pairs={{1,0},{2,1},{3,2},{4,3},{5,4},{6,5},{7,6},{8,7},{9,8},{10,9},{11,1... | collective-permute-start | bytes 442376 | tf_op jit(solution)/shard_map/ppermute | solution.py:21
  28.0 0.9 copy-start.2
  28.0 0.9 copy-start.7
  28.0 0.9 copy-start.8
  32.1 1.2 copy-start.3
  32.1 1.2 copy-start.4
  32.1 1.4 copy-start.6
  33.5 1.3 copy-start.5
  34.8 2.5 copy-start.9
  43.4 354.3 %reduce-scatter.7.cloned.1.call-start = ((), (), s32[]{:S(2)}) async-start(), calls=%async_computation.3 | async-start | bytes 1216512 | tf_op jit(solution)/shard_map/reduce_scatter | solution.py:119
  53.8 25.2 %collective-permute-start.2 = (bf16[1,3,64,384]{3,1,2,0:T(4,128)(2,1)S(1)}, bf16[1,3,64,384]{3,1,2,0:T(4,128)(2,1)S(1)}, u32[]{:S(2)}, u32[]{:S(2)}) collective-permute-start(bf16[1,3,64,384]{3,1,2,0:T(4,128)(2,1)S(1)} %get-tuple-element.24), channel_id=1, source_target_pairs={{0,1},{1,2},{2,3},{3,4},{4,5},{5,6},{6,7},{7,8},{8,9},{9,10},{10,1... | collective-permute-start | bytes 442376 | tf_op jit(solution)/shard_map/ppermute | solution.py:19
  75.0 5.1 collective-permute-start.3
  84.1 1.0 copy-start.1
Sparse Core Ops, SparseCore 0:
  43.5 190.4 reduce-scatter.4
  239.6 157.9 reduce-scatter.6
where the time goes:
time: 643 us
  waiting for transfers between devices  325 us (51%)
  blocking collectives  237 us (37%)
  starting transfers between devices  28.9 us (4%)
  matrix products  25.3 us (4%)
  between operations  15 us (2%)
  local copies, waits for them, and re-layouts  7.52 us (1%)
    unnamed x1, blocking collectives  237 us
    reduce_scatter x1, waiting for transfers between devices, on_device(): lax.psum_scatter(term_down.astype(jnp.bfloat16), 'rows', scatter_dimensio...  164 us
    reduce_scatter x1, waiting for transfers between devices, on_device(): lax.psum_scatter(term_up.astype(jnp.bfloat16), 'rows', scatter_dimension=...  148 us
    ppermute x2, starting transfers between devices, extended_2(): lax.ppermute(tail, axis, [(i, (i + 1) % count) for i in range(ends)])  23.1 us
    ppermute x2, waiting for transfers between devices, extended_2(): lax.ppermute(head, axis, [((i + 1) % count, i) for i in range(ends)])  12.9 us
  transfers between devices with their start and end apart: 6, of which 4 were waited for; matrix products, arithmetic and copies ran while one was open for 3% of the time, Pallas kernels for 0%

commit v1 on v0

--- a/solution.py
+++ b/solution.py
@@ -1,11 +1,20 @@
+import functools
 import math
 
 import jax
 import jax.numpy as jnp
 from jax import lax
+from jax.experimental import pallas as pl
+from jax.experimental.pallas import tpu as pltpu
 from jax.sharding import PartitionSpec as P
 
 EPSILON = 1e-06
+MESH = pl.DeviceIdType.MESH
+F32 = jnp.float32
+BF16 = jnp.bfloat16
+
+NZH, NX, NC, NY, NZL = 4, 4, 2, 4, 8
+HB, CB = 48, 12
 
 
 def extended_2(cells, sides, width):
@@ -43,6 +52,310 @@
     return normal_cdf + values * density
 
 
+def coordinates():
+    dp, rows = lax.axis_index("dp"), lax.axis_index("rows")
+    core, chip = lax.rem(rows, NC), lax.div(rows, NC)
+    return (
+        lax.div(chip, NX),
+        lax.rem(chip, NX),
+        core,
+        lax.div(dp, NZL),
+        lax.rem(dp, NZL),
+    )
+
+
+def device(zh, x, c, y, zl):
+    return (y * NZL + zl, (zh * NX + x) * NC + c)
+
+
+def around(place, step, count):
+    return lax.rem(place + step, count)
+
+
+class Peers:
+    def __init__(self):
+        self.at = coordinates()
+
+    def core(self):
+        zh, x, c, y, zl = self.at
+        return device(zh, x, 1 - c, y, zl)
+
+    def x(self, k):
+        zh, x, c, y, zl = self.at
+        to = around(x, k, NX)
+        return to, device(zh, to, c, y, zl)
+
+    def y(self, k):
+        zh, x, c, y, zl = self.at
+        to = around(y, k, NY)
+        return to, device(zh, x, c, to, zl)
+
+    def zl(self, k):
+        zh, x, c, y, zl = self.at
+        to = around(zl, k, NZL)
+        return to, device(zh, x, c, y, to)
+
+    def zh(self, k):
+        zh, x, c, y, zl = self.at
+        to = around(zh, k, NZH)
+        return to, device(to, x, c, y, zl)
+
+    def all(self):
+        found = [self.core()]
+        for way, count in ((self.x, NX), (self.y, NY), (self.zl, NZL), (self.zh, NZH)):
+            found += [way(k)[1] for k in range(1, count)]
+        return found
+
+
+def greet(others):
+    barrier = pltpu.get_barrier_semaphore()
+    for other in others:
+        pl.semaphore_signal(barrier, inc=1, device_id=other, device_id_type=MESH)
+    pl.semaphore_wait(barrier, len(others))
+
+
+def send(src, dst, send_sem, recv_sem, to):
+    return pltpu.make_async_remote_copy(
+        src_ref=src, dst_ref=dst, send_sem=send_sem, recv_sem=recv_sem, device_id=to, device_id_type=MESH
+    )
+
+
+def spread_channels(values):
+    width = NZL * CB
+    rows = lax.broadcasted_iota(jnp.int32, (NY * width, NY * 128), 0)
+    cols = lax.broadcasted_iota(jnp.int32, (NY * width, NY * 128), 1)
+    block, lane = cols // 128, cols % 128
+    chosen = jnp.where((lane < width) & (rows == block * width + lane), 1.0, 0.0).astype(BF16)
+    return jnp.dot(values, chosen, preferred_element_type=F32).astype(BF16)
+
+
+def reduce_scratch():
+    lanes = NY * 128
+    return dict(
+        own=pltpu.VMEM((2, NZH, NX, HB, lanes), F32),
+        b1=pltpu.VMEM((2, NZH, NX, HB, lanes), BF16),
+        r1=pltpu.VMEM((2, NZH, NX, HB, lanes), BF16),
+        b2d=pltpu.VMEM((NX, NZH, HB, lanes), BF16),
+        r2d=pltpu.VMEM((NX - 1, NZH, HB, lanes), BF16),
+        b2u=pltpu.VMEM((NY, NZH, NX, HB, 128), BF16),
+        r2u=pltpu.VMEM((NY - 1, NZH, NX, HB, 128), BF16),
+        a3u=pltpu.VMEM((NX, NZH, HB, 128), F32),
+        b3d=pltpu.VMEM((NY, NZH, HB, 128), BF16),
+        r3d=pltpu.VMEM((NY - 1, NZH, HB, 128), BF16),
+        b3u=pltpu.VMEM((NX, NZH, HB, 128), BF16),
+        r3u=pltpu.VMEM((NX - 1, NZH, HB, 128), BF16),
+        b4=pltpu.VMEM((NZL, NZH, 16, 128), BF16),
+        r4=pltpu.VMEM((NZL - 1, NZH, 16, 128), BF16),
+        a5=pltpu.VMEM((NZH, 16, 128), F32),
+        b5=pltpu.VMEM((NZH, 16, 128), BF16),
+        r5=pltpu.VMEM((NZH - 1, 16, 128), BF16),
+        s1=pltpu.SemaphoreType.DMA((2, 2, NZH)),
+        s2d=pltpu.SemaphoreType.DMA((2, NX - 1, NZH)),
+        s2u=pltpu.SemaphoreType.DMA((2, NY - 1, NZH)),
+        s3d=pltpu.SemaphoreType.DMA((2, NY - 1)),
+        s3u=pltpu.SemaphoreType.DMA((2, NX - 1)),
+        s4=pltpu.SemaphoreType.DMA((2, NZL - 1)),
+        s5=pltpu.SemaphoreType.DMA((2, NZH - 1)),
+    )
+
+
+DOWN, UP = 0, 1
+
+
+class Reduction:
+    def __init__(self, peers, refs):
+        self.peers = peers
+        self.__dict__.update(refs)
+
+    def first_copy(self, g, z):
+        return send(self.b1.at[g, z], self.r1.at[g, z], self.s1.at[0, g, z], self.s1.at[1, g, z], self.peers.core())
+
+    def term(self, g, z, left, right):
+        core = self.peers.at[2]
+        value = lax.dot_general(left, right, (((0,), (0,)), ((), ())), preferred_element_type=F32)
+        value = value.reshape(NX, NC, HB, NY * 128)
+        self.own[g, z] = jnp.where(core == 0, value[:, 0], value[:, 1])
+        self.b1[g, z] = jnp.where(core == 0, value[:, 1], value[:, 0]).astype(BF16)
+        self.first_copy(g, z).start()
+
+    def second_copies(self, g, z):
+        p = self.peers
+        if g == DOWN:
+            for k in range(1, NX):
+                to, there = p.x(k)
+                yield send(self.b2d.at[to, z], self.r2d.at[k - 1, z], self.s2d.at[0, k - 1, z], self.s2d.at[1, k - 1, z], there)
+        else:
+            for k in range(1, NY):
+                to, there = p.y(k)
+                yield send(self.b2u.at[to, z], self.r2u.at[k - 1, z], self.s2u.at[0, k - 1, z], self.s2u.at[1, k - 1, z], there)
+
+    def second(self, g, z):
+        self.first_copy(g, z).wait_recv()
+        value = self.own[g, z] + self.r1[g, z].astype(F32)
+        self.own[g, z] = value
+        if g == DOWN:
+            for x in range(NX):
+                self.b2d[x, z] = value[x].astype(BF16)
+        else:
+            for y in range(NY):
+                self.b2u[y, z] = value[:, :, y * 128 : (y + 1) * 128].astype(BF16)
+        for copy in self.second_copies(g, z):
+            copy.start()
+
+    def third_copies(self, g):
+        p = self.peers
+        if g == DOWN:
+            for k in range(1, NY):
+                to, there = p.y(k)
+                yield send(self.b3d.at[to], self.r3d.at[k - 1], self.s3d.at[0, k - 1], self.s3d.at[1, k - 1], there)
+        else:
+            for k in range(1, NX):
+                to, there = p.x(k)
+                yield send(self.b3u.at[to], self.r3u.at[k - 1], self.s3u.at[0, k - 1], self.s3u.at[1, k - 1], there)
+
+    def third_sum(self, g, z):
+        zh, x, c, y, zl = self.peers.at
+        for copy in self.second_copies(g, z):
+            copy.wait_recv()
+        if g == DOWN:
+            value = self.own[g, z, x]
+            for k in range(NX - 1):
+                value = value + self.r2d[k, z].astype(F32)
+            self.own[g, z, x] = value
+            for j in range(NY):
+                self.b3d[j, z] = value[:, j * 128 : (j + 1) * 128].astype(BF16)
+        else:
+            value = self.own[g, z, :, :, pl.ds(pl.multiple_of(y * 128, 128), 128)]
+            for k in range(NY - 1):
+                value = value + self.r2u[k, z].astype(F32)
+            for j in range(NX):
+                self.a3u[j, z] = value[j]
+                self.b3u[j, z] = value[j].astype(BF16)
+
+    def third(self, g):
+        @pl.loop(0, NZH)
+        def _(z):
+            self.third_sum(g, z)
+
+        for copy in self.third_copies(g):
+            copy.start()
+
+    def fourth_copies(self):
+        for k in range(1, NZL):
+            to, there = self.peers.zl(k)
+            yield send(self.b4.at[to], self.r4.at[k - 1], self.s4.at[0, k - 1], self.s4.at[1, k - 1], there)
+
+    def fourth(self):
+        zh, x, c, y, zl = self.peers.at
+        for g in (DOWN, UP):
+            for copy in self.third_copies(g):
+                copy.wait_recv()
+        shape = (NZL * 16, 128)
+        rows, cols = lax.broadcasted_iota(jnp.int32, shape, 0), lax.broadcasted_iota(jnp.int32, shape, 1)
+        chosen = jnp.where((rows % 16 < CB) & (cols == (rows // 16) * CB + rows % 16), 1.0, 0.0).astype(BF16)
+
+        @pl.loop(0, NZH)
+        def _(z):
+            up = self.a3u[x, z]
+            for k in range(NX - 1):
+                up = up + self.r3u[k, z].astype(F32)
+            down = self.own[DOWN, z, x, :, pl.ds(pl.multiple_of(y * 128, 128), 128)]
+            for k in range(NY - 1):
+                down = down + self.r3d[k, z].astype(F32)
+            both = jnp.concatenate([up, down, jnp.zeros((128 - 2 * HB, 128), F32)], axis=0).astype(BF16)
+            placed = lax.dot_general(chosen, both, (((1,), (1,)), ((), ())), preferred_element_type=F32)
+            placed = placed.reshape(NZL, 16, 128).astype(BF16)
+            for j in range(NZL):
+                self.b4[j, z] = placed[j]
+
+        for copy in self.fourth_copies():
+            copy.start()
+
+    def fifth_copies(self):
+        for k in range(1, NZH):
+            to, there = self.peers.zh(k)
+            yield send(self.b5.at[to], self.r5.at[k - 1], self.s5.at[0, k - 1], self.s5.at[1, k - 1], there)
+
+    def fifth(self):
+        zl = self.peers.at[4]
+        value = self.b4[zl].astype(F32)
+        for k, copy in enumerate(self.fourth_copies()):
+            copy.wait_recv()
+            value = value + self.r4[k].astype(F32)
+        self.a5[...] = value
+        self.b5[...] = value.astype(BF16)
+        for copy in self.fifth_copies():
+            copy.start()
+
+    def finish(self, factor, up_ref, down_ref):
+        zh = self.peers.at[0]
+        value = self.a5[zh]
+        for k, copy in enumerate(self.fifth_copies()):
+            copy.wait_recv()
+            value = value + self.r5[k].astype(F32)
+        value = value * factor
+        up_ref[...] = value[:CB, :HB]
+        down_ref[...] = pltpu.roll(value, 128 - HB, 1)[:CB, :HB]
+
+    def drain(self):
+        @pl.loop(0, NZH)
+        def _(z):
+            for g in (DOWN, UP):
+                self.first_copy(g, z).wait_send()
+                for copy in self.second_copies(g, z):
+                    copy.wait_send()
+
+        for g in (DOWN, UP):
+            for copy in self.third_copies(g):
+                copy.wait_send()
+        for copy in self.fourth_copies():
+            copy.wait_send()
+        for copy in self.fifth_copies():
+            copy.wait_send()
+
+
+def sums_kernel(factor, names, scaled_ref, activated_ref, normed_ref, slope_ref, up_ref, down_ref, *scratch):
+    peers = Peers()
+    sums = Reduction(peers, dict(zip(names, scratch)))
+    greet(peers.all())
+    rows = NX * NC * HB
+    for g, left_ref, right_ref in ((DOWN, activated_ref, scaled_ref), (UP, slope_ref, normed_ref)):
+        right = spread_channels(right_ref[...])
+
+        @pl.loop(0, NZH)
+        def _(z, g=g, left_ref=left_ref, right=right):
+            sums.term(g, z, left_ref[:, pl.ds(pl.multiple_of(z * rows, rows), rows)], right)
+
+    for g in (DOWN, UP):
+
+        @pl.loop(0, NZH)
+        def _(z, g=g):
+            sums.second(g, z)
+
+    for g in (DOWN, UP):
+        sums.third(g)
+    sums.fourth()
+    sums.fifth()
+    sums.finish(factor, up_ref, down_ref)
+    sums.drain()
+
+
+def weight_sums(factor, scaled, activated, normed, grad_before):
+    scratch = reduce_scratch()
+    block = jax.ShapeDtypeStruct((CB, HB), F32)
+    vmem = pl.BlockSpec(memory_space=pltpu.VMEM)
+    return pl.pallas_call(
+        functools.partial(sums_kernel, factor, tuple(scratch)),
+        out_shape=(block, block),
+        in_specs=[vmem] * 4,
+        out_specs=(vmem, vmem),
+        scratch_shapes=list(scratch.values()),
+        compiler_params=pltpu.CompilerParams(
+            collective_id=0, has_side_effects=True, vmem_limit_bytes=48 * 1024 * 1024
+        ),
+    )(scaled, activated, normed, grad_before)
+
+
 def block_terms(
     conv_out, norm_gain, norm_shift, up_weight, up_bias, down_weight, layer_scale, cotangent
 ):
@@ -55,13 +368,7 @@
     activated = jax.nn.gelu(before, approximate=False).astype(jnp.bfloat16)
     scaled = (cotangent.astype(jnp.float32) * layer_scale).astype(jnp.bfloat16)
     grad_act = jnp.dot(scaled, down_weight, preferred_element_type=jnp.float32)
-    term_down = lax.dot_general(
-        scaled, activated, (((0,), (0,)), ((), ())), preferred_element_type=jnp.float32
-    )
     grad_before = (grad_act * gelu_slope(before)).astype(jnp.bfloat16)
-    term_up = lax.dot_general(
-        normed, grad_before, (((0,), (0,)), ((), ())), preferred_element_type=jnp.float32
-    )
     grad_normed = lax.dot_general(
         grad_before, up_weight, (((1,), (1,)), ((), ())), preferred_element_type=jnp.float32
     )
@@ -71,7 +378,7 @@
         - jnp.mean(gscaled, axis=1, keepdims=True)
         - standard * jnp.mean(gscaled * standard, axis=1, keepdims=True)
     )
-    return (grad_conv.astype(jnp.bfloat16), term_up, term_down)
+    return (grad_conv.astype(jnp.bfloat16), scaled, activated, normed, grad_before)
 
 
 def on_device(
@@ -93,7 +400,7 @@
     extended = extended_2(images, (("rows", 1),), reach)
     padded = jnp.pad(extended.astype(jnp.float32), side_pad)
     conv_out = depthwise(padded, kernel) + conv_bias
-    grad_conv, term_up, term_down = block_terms(
+    grad_conv, scaled, activated, normed, grad_before = block_terms(
         conv_out.reshape(-1, channels),
         norm_gain,
         norm_shift,
@@ -110,20 +417,7 @@
     groups = lax.axis_size("dp")
     parts = lax.axis_size("rows")
     factor = 1.0 / math.sqrt(shape[0] * shape[1] * shape[2] * groups * parts)
-    term_up = term_up * factor
-    term_down = term_down * factor
-    halves = (
-        lax.psum_scatter(
-            term_up.astype(jnp.bfloat16), "rows", scatter_dimension=1, tiled=True
-        ).astype(jnp.float32),
-        lax.psum_scatter(
-            term_down.astype(jnp.bfloat16), "rows", scatter_dimension=1, tiled=True
-        ).astype(jnp.float32),
-    )
-    grad_up, grad_down = (
-        lax.psum_scatter(halves[0], "dp", scatter_dimension=0, tiled=True),
-        lax.psum_scatter(halves[1], "dp", scatter_dimension=0, tiled=True),
-    )
+    grad_up, grad_down = weight_sums(factor, scaled, activated, normed, grad_before)
     return (grad_images, grad_up, grad_down)
 
 

time: 643 us -> 167 us (0.26)
  the two profiles are of different devices: /device:TPU:6 before, /device:TPU:4 now
where the time goes in v1:
time: 167 us
  Pallas kernels  106 us (63%)
  matrix products  23.2 us (14%)
  starting transfers between devices  11.5 us (7%)
  other arithmetic  11 us (7%)
  local copies, waits for them, and re-layouts  10.7 us (6%)
  waiting for transfers between devices  2.75 us (2%)
    pallas_call x1, Pallas kernels, weight_sums(): pl.pallas_call(functools.partial(sums_kernel, factor, tuple(scratch)), ou...  106 us
    conv_general_dilated x2, matrix products, depthwise(): lax.conv_general_dilated(padded, kernel[:, :, None, :], (1, 1), 'VALID',...  11.7 us
    dot_general x1, matrix products, block_terms(): jnp.dot(normed, up_weight, preferred_element_type=jnp.float32) + up_bias  8.78 us
    reduce_sum x1, other arithmetic, block_terms(): jnp.mean(centered * centered, axis=1, keepdims=True) + EPSILON  7.41 us
    ppermute x2, starting transfers between devices, extended_2(): lax.ppermute(head, axis, [((i + 1) % count, i) for i in range(ends)])  6.18 us
    unnamed x37, local copies, waits for them, and re-layouts  6.01 us
    ppermute x2, starting transfers between devices, extended_2(): lax.ppermute(tail, axis, [(i, (i + 1) % count) for i in range(ends)])  5.29 us
  transfers between devices with their start and end apart: 4, of which 2 were waited for; matrix products, arithmetic and copies ran while one was open for 2% of the time, Pallas kernels for 64%

profile of v1, /device:TPU:4, one launch (start us, length us, event | category | flops | bytes accessed | tf_op | source)
XLA Modules:
  0.0 166.6 jit_solution(2047999923553275354)
XLA Ops:
  0.7 1.7 %copy.19 = bf16[1,8,64,384]{3,0,2,1:T(2,128)(2,1)S(1)} copy(bf16[1,8,64,384]{3,2,1,0:T(8,128)(2,1)} %param.10) | data formatting | bytes 786432 | tf_op args[0]
  2.4 0.6 fusion.47
  3.0 1.9 %collective-permute-start = (bf16[1,3,64,384]{3,0,2,1:T(2,128)(2,1)S(1)}, bf16[1,3,64,384]{3,0,2,1:T(2,128)(2,1)S(1)}, u32[]{:S(2)}, u32[]{:S(2)}) collective-permute-start(bf16[1,3,64,384]{3,0,2,1:T(2,128)(2,1)S(1)} %get-tuple-element.12), channel_id=1, source_target_pairs={{0,1},{1,2},{2,3},{3,4},{4,5},{5,6},{6,7},{7,8},{8,9},{9,10},{10,1... | collective-permute-start | bytes 442376 | tf_op jit(solution)/shard_map/ppermute | solution.py:28
  5.0 3.6 %collective-permute-start.1 = (bf16[1,3,64,384]{3,0,2,1:T(2,128)(2,1)S(1)}, bf16[1,3,64,384]{3,0,2,1:T(2,128)(2,1)S(1)}, u32[]{:S(2)}, u32[]{:S(2)}) collective-permute-start(bf16[1,3,64,384]{3,0,2,1:T(2,128)(2,1)S(1)} %get-tuple-element.13), channel_id=1, source_target_pairs={{1,0},{2,1},{3,2},{4,3},{5,4},{6,5},{7,6},{8,7},{9,8},{10,9},{11,1... | collective-permute-start | bytes 442376 | tf_op jit(solution)/shard_map/ppermute | solution.py:30
  8.6 1.2 copy_convert_fusion
  10.1 1.0 collective-permute-done
  11.1 1.8 %collective-permute-done.1 = bf16[1,3,64,384]{3,0,2,1:T(2,128)(2,1)S(1)} collective-permute-done((bf16[1,3,64,384]{3,0,2,1:T(2,128)(2,1)S(1)}, bf16[1,3,64,384]{3,0,2,1:T(2,128)(2,1)S(1)}, u32[]{:S(2)}, u32[]{:S(2)}) %collective-permute-start.1) | collective-permute-done | bytes 147488 | tf_op jit(solution)/shard_map/ppermute | solution.py:30
  12.9 8.5 %fusion.49 = (f32[8,64]{1,0:T(8,128)S(1)}, f32[1,8,64,384]{3,0,2,1:T(1,128)S(1)}) fusion(f32[384]{0:T(512)S(1)} %copy-done.14, f32[7,7,1,384]{3,1,0,2:T(8,128)S(1)} %bitcast.41, bf16[1,3,64,384]{3,0,2,1:T(2,128)(2,1)S(1)} %collective-permute-done.1, bf16[1,8,64,384]{3,0,2,1:T(2,128)(2,1)S(1)} %copy.19, bf16[1,3,64,384]{3,0,2,1:T(2,128)(2,1)S(1)} %collective-permute-done), kind=kOutput, calls=%fused_computation.71 | convolution fusion | flops 114966016 | bytes 1553408 | tf_op jit(solution)/shard_map/conv_general_dilated | solution.py:38
  21.5 7.4 %multiply_reduce_fusion.1 = f32[8,64]{1,0:T(8,128)S(1)} fusion(f32[1,8,64,384]{3,0,2,1:T(1,128)S(1)} %get-tuple-element.17, f32[8,64]{1,0:T(8,128)S(1)} %broadcast_multiply_fusion), kind=kLoop, calls=%fused_computation.55 | loop fusion | flops 589312 | bytes 790528 | tf_op jit(solution)/shard_map/reduce_sum | solution.py:364
  29.3 8.8 %fusion.6 = (bf16[512,1536]{1,0:T(8,128)(2,1)S(1)}, f32[512,1536]{1,0:T(8,128)S(1)}) fusion(f32[1536]{0:T(1024)} %param.16, bf16[512,384]{1,0:T(8,128)(2,1)S(1)} %add_convert_fusion.normed_ref, bf16[384,1536]{1,0:T(8,128)(2,1)S(1)} %copy-done), kind=kOutput, calls=%fused_computation.10 | convolution fusion | flops 655884288 | bytes 6297600 | tf_op jit(solution)/shard_map/dot_general | solution.py:367
  38.1 1.6 fusion.14.slope_ref
  39.8 1.1 fusion.46
  41.5 0.7 copy-done.5
  42.2 0.9 fusion.48
  43.1 3.4 %collective-permute-start.2 = (bf16[1,3,64,384]{3,1,2,0:T(4,128)(2,1)}, bf16[1,3,64,384]{3,1,2,0:T(4,128)(2,1)}, u32[]{:S(2)}, u32[]{:S(2)}) collective-permute-start(bf16[1,3,64,384]{3,1,2,0:T(4,128)(2,1)} %get-tuple-element.14), channel_id=1, source_target_pairs={{0,1},{1,2},{2,3},{3,4},{4,5},{5,6},{6,7},{7,8},{8,9},{9,10},{10,1... | collective-permute-start | bytes 442376 | tf_op jit(solution)/shard_map/ppermute | solution.py:28
  46.5 2.5 %collective-permute-start.3 = (bf16[1,3,64,384]{3,1,2,0:T(4,128)(2,1)}, bf16[1,3,64,384]{3,1,2,0:T(4,128)(2,1)}, u32[]{:S(2)}, u32[]{:S(2)}) collective-permute-start(bf16[1,3,64,384]{3,1,2,0:T(4,128)(2,1)} %get-tuple-element.15), channel_id=1, source_target_pairs={{1,0},{2,1},{3,2},{4,3},{5,4},{6,5},{7,6},{8,7},{9,8},{10,9},{11,1... | collective-permute-start | bytes 442376 | tf_op jit(solution)/shard_map/ppermute | solution.py:30
  49.0 2.1 %rev.3 = f32[7,7,384]{2,1,0:T(8,128)} reverse(f32[7,7,384]{2,1,0:T(8,128)} %param.11), dimensions={0,1} | reverse | bytes 150528 | tf_op jit(solution)/shard_map/rev | solution.py:415
  51.2 1.4 copy-done.2
  52.6 106.4 %shard_map.121 = (f32[12,48]{1,0:T(8,128)S(1)}, f32[12,48]{1,0:T(8,128)S(1)}) custom-call(bf16[512,384]{1,0:T(8,128)(2,1)S(1)} %fusion.38.scaled_ref, bf16[512,1536]{1,0:T(8,128)(2,1)S(1)} %get-tuple-element.19.activated_ref, bf16[512,384]{1,0:T(8,128)(2,1)S(1)} %add_convert_fusion.normed_ref, bf16[512,1536]{1,0:T(8,128)(2,1)S(1)} %copy-done.2), custom_call_target="tpu_custom_call" | custom-call | tf_op jit(solution)/shard_map/pallas_call | solution.py:347
  159.1 1.5 maximum_bitcast_fusion
  161.0 3.2 %fusion.29 = f32[8,8,9,384]{3,1,2,0:T(8,128)S(1)} fusion(bf16[14,1,7,6,384]{4,2,3,0,1:T(8,128)(2,1)S(1)} %slice.22, bf16[14,1,8,9,384]{4,2,3,0,1:T(8,128)(2,1)S(1)} %copy.28, pred[8,9]{0,1:T(8,128)(4,1)S(1)} %copy-done.15, f32[7,7,1,384]{3,1,0,2:T(8,128)S(1)} %bitcast.42), kind=kOutput, calls=%fused_computation.42 | convolution fusion | flops 134148096 | bytes 2185800 | tf_op jit(solution)/shard_map/conv_general_dilated | solution.py:38
  164.6 0.8 copy.31
  165.4 0.6 copy.44
  166.0 0.6 copy.45
  (48 shorter events, 2.2 us)
Async XLA Ops:
  0.6 28.7 %copy-start = (bf16[384,1536]{1,0:T(8,128)(2,1)S(1)}, bf16[384,1536]{1,0:T(8,128)(2,1)}, u32[]{:S(2)}) copy-start(bf16[384,1536]{1,0:T(8,128)(2,1)} %param.15) | copy-start | bytes 3538948
  0.6 9.4 %copy-start.10 = (f32[384]{0:T(512)S(1)}, f32[384]{0:T(512)}, u32[]{:S(2)}) copy-start(f32[384]{0:T(512)} %param.18) | copy-start | bytes 4612
  0.7 12.2 %copy-start.8 = (f32[7,7,384]{2,1,0:T(8,128)S(1)}, f32[7,7,384]{2,1,0:T(8,128)}, u32[]{:S(2)}) copy-start(f32[7,7,384]{2,1,0:T(8,128)} %param.11) | copy-start | bytes 225796
  0.7 12.2 %copy-start.14 = (f32[384]{0:T(512)S(1)}, f32[384]{0:T(512)}, u32[]{:S(2)}) copy-start(f32[384]{0:T(512)} %param.12) | copy-start | bytes 4612
  3.0 8.0 %collective-permute-start = (bf16[1,3,64,384]{3,0,2,1:T(2,128)(2,1)S(1)}, bf16[1,3,64,384]{3,0,2,1:T(2,128)(2,1)S(1)}, u32[]{:S(2)}, u32[]{:S(2)}) collective-permute-start(bf16[1,3,64,384]{3,0,2,1:T(2,128)(2,1)S(1)} %get-tuple-element.12), channel_id=1, source_target_pairs={{0,1},{1,2},{2,3},{3,4},{4,5},{5,6},{6,7},{7,8},{8,9},{9,10},{10,1... | collective-permute-start | bytes 442376 | tf_op jit(solution)/shard_map/ppermute | solution.py:28
  5.0 7.9 %collective-permute-start.1 = (bf16[1,3,64,384]{3,0,2,1:T(2,128)(2,1)S(1)}, bf16[1,3,64,384]{3,0,2,1:T(2,128)(2,1)S(1)}, u32[]{:S(2)}, u32[]{:S(2)}) collective-permute-start(bf16[1,3,64,384]{3,0,2,1:T(2,128)(2,1)S(1)} %get-tuple-element.13), channel_id=1, source_target_pairs={{1,0},{2,1},{3,2},{4,3},{5,4},{6,5},{7,6},{8,7},{9,8},{10,9},{11,1... | collective-permute-start | bytes 442376 | tf_op jit(solution)/shard_map/ppermute | solution.py:30
  12.8 16.2 %copy-start.11 = (f32[384]{0:T(512)S(1)}, f32[384]{0:T(512)}, u32[]{:S(2)}) copy-start(f32[384]{0:T(512)} %param.14) | copy-start | bytes 4612
  12.8 16.2 %copy-start.12 = (f32[384]{0:T(512)S(1)}, f32[384]{0:T(512)}, u32[]{:S(2)}) copy-start(f32[384]{0:T(512)} %param.13) | copy-start | bytes 4612
  21.5 7.6 %copy-start.3 = (f32[1,8,64,384]{3,2,0,1:T(8,128)}, f32[1,8,64,384]{3,2,0,1:T(8,128)S(1)}, u32[]{:S(2)}) copy-start(f32[1,8,64,384]{3,2,0,1:T(8,128)S(1)} %copy.32) | copy-start | bytes 2359300
  29.3 8.8 %copy-start.13 = (bf16[384,1536]{1,0:T(8,128)(2,1)S(1)}, bf16[384,1536]{1,0:T(8,128)(2,1)}, u32[]{:S(2)}) copy-start(bf16[384,1536]{1,0:T(8,128)(2,1)} %param.17) | copy-start | bytes 3538948
  38.1 1.6 copy-start.4
  39.7 1.5 copy-start.1
  41.5 0.7 copy-start.5
  43.1 115.9 %collective-permute-start.2 = (bf16[1,3,64,384]{3,1,2,0:T(4,128)(2,1)}, bf16[1,3,64,384]{3,1,2,0:T(4,128)(2,1)}, u32[]{:S(2)}, u32[]{:S(2)}) collective-permute-start(bf16[1,3,64,384]{3,1,2,0:T(4,128)(2,1)} %get-tuple-element.14), channel_id=1, source_target_pairs={{0,1},{1,2},{2,3},{3,4},{4,5},{5,6},{6,7},{7,8},{8,9},{9,10},{10,1... | collective-permute-start | bytes 442376 | tf_op jit(solution)/shard_map/ppermute | solution.py:28
  46.5 112.6 %collective-permute-start.3 = (bf16[1,3,64,384]{3,1,2,0:T(4,128)(2,1)}, bf16[1,3,64,384]{3,1,2,0:T(4,128)(2,1)}, u32[]{:S(2)}, u32[]{:S(2)}) collective-permute-start(bf16[1,3,64,384]{3,1,2,0:T(4,128)(2,1)} %get-tuple-element.15), channel_id=1, source_target_pairs={{1,0},{2,1},{3,2},{4,3},{5,4},{6,5},{7,6},{8,7},{9,8},{10,9},{11,1... | collective-permute-start | bytes 442376 | tf_op jit(solution)/shard_map/ppermute | solution.py:30
  51.2 1.4 copy-start.2
  52.6 106.5 %copy-start.6 = (bf16[1,8,64,384]{3,1,2,0:T(8,128)(2,1)S(1)}, bf16[1,8,64,384]{3,1,2,0:T(8,128)(2,1)}, u32[]{:S(2)}) copy-start(bf16[1,8,64,384]{3,1,2,0:T(8,128)(2,1)} %copy-done.5) | copy-start | bytes 1179652
  159.0 2.0 %copy-start.9 = (f32[7,7,384]{2,1,0:T(8,128)S(1)}, f32[7,7,384]{2,1,0:T(8,128)}, u32[]{:S(2)}) copy-start(f32[7,7,384]{2,1,0:T(8,128)} %rev.3) | copy-start | bytes 225796
  159.0 2.0 %copy-start.15 = (pred[8,9]{0,1:T(8,128)(4,1)S(1)}, pred[8,9]{0,1:T(8,128)(4,1)}, u32[]{:S(2)}) copy-start(pred[8,9]{0,1:T(8,128)(4,1)} %constant.85) | copy-start | bytes 220
  161.0 3.3 %copy-start.7 = (bf16[1,8,64,384]{3,2,1,0:T(8,128)(2,1)S(1)}, bf16[1,8,64,384]{3,2,1,0:T(8,128)(2,1)}, u32[]{:S(2)}) copy-start(bf16[1,8,64,384]{3,2,1,0:T(8,128)(2,1)} %param.19) | copy-start | bytes 1179652

commit v2 on v1

--- a/solution.py
+++ b/solution.py
@@ -14,42 +14,8 @@
 BF16 = jnp.bfloat16
 
 NZH, NX, NC, NY, NZL = 4, 4, 2, 4, 8
+NROWS = NZH * NX * NC
 HB, CB = 48, 12
-
-
-def extended_2(cells, sides, width):
-    for axis, dim in sides:
-        count = lax.axis_size(axis)
-        ends = count - 1
-        head = lax.slice_in_dim(cells, 0, width, axis=dim)
-        tail = lax.slice_in_dim(cells, cells.shape[dim] - width, cells.shape[dim], axis=dim)
-        cells = jnp.concatenate(
-            [
-                lax.ppermute(tail, axis, [(i, (i + 1) % count) for i in range(ends)]),
-                cells,
-                lax.ppermute(head, axis, [((i + 1) % count, i) for i in range(ends)]),
-            ],
-            axis=dim,
-        )
-    return cells
-
-
-def depthwise(padded, kernel):
-    return lax.conv_general_dilated(
-        padded,
-        kernel[:, :, None, :],
-        (1, 1),
-        "VALID",
-        dimension_numbers=("NHWC", "HWIO", "NHWC"),
-        feature_group_count=kernel.shape[2],
-        precision=lax.Precision.HIGHEST,
-    )
-
-
-def gelu_slope(values):
-    normal_cdf = 0.5 * (1.0 + jax.scipy.special.erf(values * (1.0 / math.sqrt(2.0))))
-    density = jnp.exp(-0.5 * values * values) * (1.0 / math.sqrt(2.0 * math.pi))
-    return normal_cdf + values * density
 
 
 def coordinates():
@@ -97,12 +63,17 @@
 
     def zh(self, k):
         zh, x, c, y, zl = self.at
-        to = around(zh, k, NZH)
+        to = zh + 1 - 2 * lax.rem(zh, 2) if k == 0 else NZH - 1 - zh
         return to, device(to, x, c, y, zl)
 
+    def strip(self, step):
+        zh, x, c, y, zl = self.at
+        row = around((zh * NX + x) * NC + c, step + NROWS, NROWS)
+        return (y * NZL + zl, row)
+
     def all(self):
-        found = [self.core()]
-        for way, count in ((self.x, NX), (self.y, NY), (self.zl, NZL), (self.zh, NZH)):
+        found = [self.core(), self.strip(-1), self.strip(1), self.zh(0)[1], self.zh(1)[1]]
+        for way, count in ((self.x, NX), (self.y, NY), (self.zl, NZL)):
             found += [way(k)[1] for k in range(1, count)]
         return found
 
@@ -111,7 +82,10 @@
     barrier = pltpu.get_barrier_semaphore()
     for other in others:
         pl.semaphore_signal(barrier, inc=1, device_id=other, device_id_type=MESH)
-    pl.semaphore_wait(barrier, len(others))
+
+
+def await_greetings(others):
+    pl.semaphore_wait(pltpu.get_barrier_semaphore(), len(others))
 
 
 def send(src, dst, send_sem, recv_sem, to):
@@ -148,14 +122,16 @@
         r4=pltpu.VMEM((NZL - 1, NZH, 16, 128), BF16),
         a5=pltpu.VMEM((NZH, 16, 128), F32),
         b5=pltpu.VMEM((NZH, 16, 128), BF16),
-        r5=pltpu.VMEM((NZH - 1, 16, 128), BF16),
+        b6=pltpu.VMEM((16, 128), BF16),
+        r5=pltpu.VMEM((3, 16, 128), BF16),
+        total=pltpu.VMEM((2, NZH, NX * NC * HB, lanes), F32),
         s1=pltpu.SemaphoreType.DMA((2, 2, NZH)),
         s2d=pltpu.SemaphoreType.DMA((2, NX - 1, NZH)),
         s2u=pltpu.SemaphoreType.DMA((2, NY - 1, NZH)),
         s3d=pltpu.SemaphoreType.DMA((2, NY - 1)),
         s3u=pltpu.SemaphoreType.DMA((2, NX - 1)),
         s4=pltpu.SemaphoreType.DMA((2, NZL - 1)),
-        s5=pltpu.SemaphoreType.DMA((2, NZH - 1)),
+        s5=pltpu.SemaphoreType.DMA((2, 3)),
     )
 
 
@@ -170,13 +146,20 @@
     def first_copy(self, g, z):
         return send(self.b1.at[g, z], self.r1.at[g, z], self.s1.at[0, g, z], self.s1.at[1, g, z], self.peers.core())
 
-    def term(self, g, z, left, right):
+    def term(self, g, z, left, right, last):
         core = self.peers.at[2]
         value = lax.dot_general(left, right, (((0,), (0,)), ((), ())), preferred_element_type=F32)
-        value = value.reshape(NX, NC, HB, NY * 128)
-        self.own[g, z] = jnp.where(core == 0, value[:, 0], value[:, 1])
-        self.b1[g, z] = jnp.where(core == 0, value[:, 1], value[:, 0]).astype(BF16)
-        self.first_copy(g, z).start()
+
+        @pl.when(jnp.logical_not(last))
+        def _():
+            self.total[g, z] = value
+
+        @pl.when(last)
+        def _():
+            whole = (value + self.total[g, z]).reshape(NX, NC, HB, NY * 128)
+            self.own[g, z] = jnp.where(core == 0, whole[:, 0], whole[:, 1])
+            self.b1[g, z] = jnp.where(core == 0, whole[:, 1], whole[:, 0]).astype(BF16)
+            self.first_copy(g, z).start()
 
     def second_copies(self, g, z):
         p = self.peers
@@ -272,9 +255,13 @@
             copy.start()
 
     def fifth_copies(self):
-        for k in range(1, NZH):
-            to, there = self.peers.zh(k)
-            yield send(self.b5.at[to], self.r5.at[k - 1], self.s5.at[0, k - 1], self.s5.at[1, k - 1], there)
+        to, there = self.peers.zh(0)
+        for k, block in enumerate((to, NZH - 1 - to)):
+            yield send(self.b5.at[block], self.r5.at[k], self.s5.at[0, k], self.s5.at[1, k], there)
+
+    def sixth_copy(self):
+        to, there = self.peers.zh(1)
+        return send(self.b6, self.r5.at[2], self.s5.at[0, 2], self.s5.at[1, 2], there)
 
     def fifth(self):
         zl = self.peers.at[4]
@@ -287,13 +274,18 @@
         for copy in self.fifth_copies():
             copy.start()
 
+    def sixth(self):
+        zh = self.peers.at[0]
+        for copy in self.fifth_copies():
+            copy.wait_recv()
+        self.b6[...] = (self.a5[NZH - 1 - zh] + self.r5[1].astype(F32)).astype(BF16)
+        self.sixth_copy().start()
+
     def finish(self, factor, up_ref, down_ref):
         zh = self.peers.at[0]
-        value = self.a5[zh]
-        for k, copy in enumerate(self.fifth_copies()):
-            copy.wait_recv()
-            value = value + self.r5[k].astype(F32)
-        value = value * factor
+        value = self.a5[zh] + self.r5[0].astype(F32)
+        self.sixth_copy().wait_recv()
+        value = (value + self.r5[2].astype(F32)) * factor
         up_ref[...] = value[:CB, :HB]
         down_ref[...] = pltpu.roll(value, 128 - HB, 1)[:CB, :HB]
 
@@ -312,73 +304,230 @@
             copy.wait_send()
         for copy in self.fifth_copies():
             copy.wait_send()
-
-
-def sums_kernel(factor, names, scaled_ref, activated_ref, normed_ref, slope_ref, up_ref, down_ref, *scratch):
+        self.sixth_copy().wait_send()
+
+
+KS, REACH = 7, 3
+HROWS, COLS = 8, 64
+HALF = HROWS // 2 * COLS
+
+
+def row_sum(rows, kernel_ref, lanes, flip):
+    col = lax.broadcasted_iota(jnp.int32, (COLS, 128), 0)
+    total = None
+    for j in range(KS):
+        part = None
+        for value, i in rows:
+            a, b = (KS - 1 - i, KS - 1 - j) if flip else (i, j)
+            tap = value * kernel_ref[a, b : b + 1, lanes]
+            part = tap if part is None else part + tap
+        shift = j - REACH
+        if shift != 0:
+            inside = (col + shift >= 0) & (col + shift < COLS)
+            part = jnp.where(inside, pltpu.roll(part, (-shift) % COLS, 0), 0.0)
+        total = part if total is None else total + part
+    return total
+
+
+def own_rows(source, sums, kernel_ref, flip):
+    @pl.loop(0, source.shape[2] // 128)
+    def _(block):
+        lanes = pl.ds(pl.multiple_of(block * 128, 128), 128)
+
+        @pl.loop(0, HROWS)
+        def _(h):
+            rows = [(source[h + i, :, lanes], i) for i in range(KS)]
+            sums[h, :, lanes] = row_sum(rows, kernel_ref, lanes, flip)
+
+
+def halo_rows(halo, side, sums, kernel_ref, flip):
+    for static_side in (0, 1):
+
+        @pl.when(side == static_side)
+        def _(static_side=static_side):
+            @pl.loop(0, sums.shape[2] // 128)
+            def _(block):
+                lanes = pl.ds(pl.multiple_of(block * 128, 128), 128)
+                rows = [halo[static_side, r * COLS : (r + 1) * COLS, lanes].astype(F32) for r in range(REACH)]
+                for h in range(REACH):
+                    if static_side == 0:
+                        used, at = [(rows[r], r - h) for r in range(h, REACH)], h
+                    else:
+                        used, at = [(rows[r], KS - 1 + r - h) for r in range(h + 1)], HROWS - REACH + h
+                    sums[at, :, lanes] = sums[at, :, lanes] + row_sum(used, kernel_ref, lanes, flip)
+
+
+def gelu_parts(values):
+    denominator = 1.0 + 0.2316419 * jnp.abs(values)
+    guess = pl.reciprocal(denominator, approx=True)
+    t = guess * (2.0 - denominator * guess)
+    density = jnp.exp2(values * values * (-0.5 * math.log2(math.e))) * (1.0 / math.sqrt(2.0 * math.pi))
+    series = t * (0.319381530 + t * (-0.356563782 + t * (1.781477937 + t * (-1.821255978 + t * 1.330274429))))
+    tail = density * series
+    cdf = jnp.where(values >= 0.0, 1.0 - tail, tail)
+    return values * cdf, cdf + values * density
+
+
+def block_kernel(factor, names, images, kernel, conv_bias, gain, shift, up_weight, up_bias, down_weight, scale, cotangent,
+                 out, up_out, down_out, *scratch):
+    s = dict(zip(names, scratch))
     peers = Peers()
-    sums = Reduction(peers, dict(zip(names, scratch)))
-    greet(peers.all())
-    rows = NX * NC * HB
-    for g, left_ref, right_ref in ((DOWN, activated_ref, scaled_ref), (UP, slope_ref, normed_ref)):
-        right = spread_channels(right_ref[...])
+    others = peers.all()
+    greet(others)
+    sums = Reduction(peers, s)
+    zh, x, c, y, zl = peers.at
+    strip = (zh * NX + x) * NC + c
+    channels, hidden = up_weight.shape
+    width = NX * NC * HB
+    source, gradient, conv = s["source"], s["gradient"], s["conv"]
+    scaled, spread_scaled, grad_act = s["scaled"], s["spread_scaled"], s["grad_act"]
+    standard, inverse, normed, spread_normed = s["standard"], s["inverse"], s["normed"], s["spread_normed"]
+    before, activated, slope, grad_normed, grad_conv = s["before"], s["activated"], s["slope"], s["grad_normed"], s["grad_conv"]
+
+    def chunk(n):
+        return pl.ds(pl.multiple_of(n * width, 128), width)
+
+    def has_neighbour(side):
+        return jnp.where(side == 0, strip > 0, strip < NROWS - 1)
+
+    def halo_copy(strip_ref, halo, sems, side):
+        first = pl.multiple_of(side * ((HROWS - REACH) * COLS), COLS)
+        return send(strip_ref.at[pl.ds(first, REACH * COLS)], halo.at[1 - side], sems.at[0, side], sems.at[1, 1 - side],
+                    peers.strip(2 * side - 1))
+
+    def arrived(strip_ref, halo, sems, side):
+        halo_copy(strip_ref, halo, sems, 1 - side).wait_recv()
+
+    for rows in (source, gradient):
+        rows[:REACH] = jnp.zeros((REACH, COLS, channels), F32)
+        rows[REACH + HROWS :] = jnp.zeros((REACH, COLS, channels), F32)
+
+    @pl.loop(0, HROWS)
+    def _(h):
+        at = pl.ds(pl.multiple_of(h * COLS, COLS), COLS)
+        source[REACH + h] = images[at, :].astype(F32)
+        scaled[at, :] = (cotangent[at, :].astype(F32) * scale[...]).astype(BF16)
+
+    own_rows(source, conv, kernel, False)
+    spread_scaled[...] = spread_channels(scaled[...])
+
+    @pl.loop(0, NZH)
+    def _(n):
+        grad_act[:, chunk(n)] = jnp.dot(scaled[...], down_weight[:, chunk(n)], preferred_element_type=F32)
+
+    await_greetings(others)
+    for side in (0, 1):
+
+        @pl.when(has_neighbour(side))
+        def _(side=side):
+            halo_copy(images, s["image_halo"], s["image_sems"], side).start()
+
+    early = jnp.where((x == 0) & (c == 0), 1, 0)
+
+    @pl.loop(0, 2)
+    def _(step):
+        half = jnp.where(step == 0, early, 1 - early)
+        last = step == 1
+
+        @pl.when(has_neighbour(half))
+        def _():
+            arrived(images, s["image_halo"], s["image_sems"], half)
+            halo_rows(s["image_halo"], half, conv, kernel, False)
+
+        pixels = pl.ds(pl.multiple_of(half * HALF, HALF), HALF)
+
+        @pl.loop(0, HROWS // 2)
+        def _(k):
+            h = half * (HROWS // 2) + k
+            at = pl.ds(pl.multiple_of(h * COLS, COLS), COLS)
+            value = conv[h] + conv_bias[...]
+            centered = value - jnp.sum(value, axis=1, keepdims=True) * (1.0 / channels)
+            inv = lax.rsqrt(jnp.sum(centered * centered, axis=1, keepdims=True) * (1.0 / channels) + EPSILON)
+            std = centered * inv
+            standard[at, :] = std
+            inverse[at, :] = inv
+            normed[at, :] = (std * gain[...] + shift[...]).astype(BF16)
+
+        spread_normed[...] = spread_channels(normed[pixels, :])
 
         @pl.loop(0, NZH)
-        def _(z, g=g, left_ref=left_ref, right=right):
-            sums.term(g, z, left_ref[:, pl.ds(pl.multiple_of(z * rows, rows), rows)], right)
+        def _(n):
+            weights = up_weight[:, chunk(n)]
+            before[...] = jnp.dot(normed[pixels, :], weights, preferred_element_type=F32)
+
+            @pl.loop(0, HALF // TILE)
+            def _(k):
+                at = pl.ds(pl.multiple_of(k * TILE, TILE), TILE)
+                act, slopes = gelu_parts(before[at, :] + up_bias[:, chunk(n)])
+                activated[at, :] = act.astype(BF16)
+                grads = grad_act[pl.ds(pl.multiple_of(half * HALF + k * TILE, TILE), TILE), chunk(n)]
+                slope[at, :] = (grads * slopes).astype(BF16)
+
+            sums.term(DOWN, n, activated[...], spread_scaled[pixels, :], last)
+            sums.term(UP, n, slope[...], spread_normed[...], last)
+            back = lax.dot_general(slope[...], weights, (((1,), (1,)), ((), ())), preferred_element_type=F32)
+
+            @pl.when(n == 0)
+            def _():
+                grad_normed[...] = back
+
+            @pl.when(n > 0)
+            def _():
+                grad_normed[...] = grad_normed[...] + back
+
+            @pl.when(last & (n > 0))
+            def _():
+                sums.second(DOWN, n - 1)
+                sums.second(UP, n - 1)
+
+        @pl.loop(0, HROWS // 2)
+        def _(k):
+            h = half * (HROWS // 2) + k
+            at = pl.ds(pl.multiple_of(h * COLS, COLS), COLS)
+            gscaled = grad_normed[pl.ds(pl.multiple_of(k * COLS, COLS), COLS), :] * gain[...]
+            std = standard[at, :]
+            mean = jnp.sum(gscaled, axis=1, keepdims=True) * (1.0 / channels)
+            along = jnp.sum(gscaled * std, axis=1, keepdims=True) * (1.0 / channels)
+            value = (inverse[at, :] * (gscaled - mean - std * along)).astype(BF16)
+            grad_conv[at, :] = value
+            gradient[REACH + h] = value.astype(F32)
+
+        @pl.when(has_neighbour(half))
+        def _():
+            halo_copy(grad_conv, s["grad_halo"], s["grad_sems"], half).start()
 
     for g in (DOWN, UP):
-
-        @pl.loop(0, NZH)
-        def _(z, g=g):
-            sums.second(g, z)
-
+        sums.second(g, NZH - 1)
+    own_rows(gradient, conv, kernel, True)
     for g in (DOWN, UP):
         sums.third(g)
     sums.fourth()
+    for step in (0, 1):
+        side = jnp.where(step == 0, early, 1 - early)
+
+        @pl.when(has_neighbour(side))
+        def _(side=side):
+            arrived(grad_conv, s["grad_halo"], s["grad_sems"], side)
+            halo_rows(s["grad_halo"], side, conv, kernel, True)
+
+    @pl.loop(0, HROWS)
+    def _(h):
+        at = pl.ds(pl.multiple_of(h * COLS, COLS), COLS)
+        out[at, :] = (cotangent[at, :].astype(F32) + conv[h]).astype(BF16)
+
     sums.fifth()
-    sums.finish(factor, up_ref, down_ref)
+    sums.sixth()
+    sums.finish(factor, up_out, down_out)
     sums.drain()
-
-
-def weight_sums(factor, scaled, activated, normed, grad_before):
-    scratch = reduce_scratch()
-    block = jax.ShapeDtypeStruct((CB, HB), F32)
-    vmem = pl.BlockSpec(memory_space=pltpu.VMEM)
-    return pl.pallas_call(
-        functools.partial(sums_kernel, factor, tuple(scratch)),
-        out_shape=(block, block),
-        in_specs=[vmem] * 4,
-        out_specs=(vmem, vmem),
-        scratch_shapes=list(scratch.values()),
-        compiler_params=pltpu.CompilerParams(
-            collective_id=0, has_side_effects=True, vmem_limit_bytes=48 * 1024 * 1024
-        ),
-    )(scaled, activated, normed, grad_before)
-
-
-def block_terms(
-    conv_out, norm_gain, norm_shift, up_weight, up_bias, down_weight, layer_scale, cotangent
-):
-    row_mean = jnp.mean(conv_out, axis=1, keepdims=True)
-    centered = conv_out - row_mean
-    inverse = lax.rsqrt(jnp.mean(centered * centered, axis=1, keepdims=True) + EPSILON)
-    standard = centered * inverse
-    normed = (standard * norm_gain + norm_shift).astype(jnp.bfloat16)
-    before = jnp.dot(normed, up_weight, preferred_element_type=jnp.float32) + up_bias
-    activated = jax.nn.gelu(before, approximate=False).astype(jnp.bfloat16)
-    scaled = (cotangent.astype(jnp.float32) * layer_scale).astype(jnp.bfloat16)
-    grad_act = jnp.dot(scaled, down_weight, preferred_element_type=jnp.float32)
-    grad_before = (grad_act * gelu_slope(before)).astype(jnp.bfloat16)
-    grad_normed = lax.dot_general(
-        grad_before, up_weight, (((1,), (1,)), ((), ())), preferred_element_type=jnp.float32
-    )
-    gscaled = grad_normed * norm_gain
-    grad_conv = inverse * (
-        gscaled
-        - jnp.mean(gscaled, axis=1, keepdims=True)
-        - standard * jnp.mean(gscaled * standard, axis=1, keepdims=True)
-    )
-    return (grad_conv.astype(jnp.bfloat16), scaled, activated, normed, grad_before)
+    for strip_ref, halo, sems in ((images, s["image_halo"], s["image_sems"]), (grad_conv, s["grad_halo"], s["grad_sems"])):
+        for side in (0, 1):
+
+            @pl.when(has_neighbour(side))
+            def _(strip_ref=strip_ref, halo=halo, sems=sems, side=side):
+                halo_copy(strip_ref, halo, sems, side).wait_send()
+
+
+TILE = 64
 
 
 def on_device(
@@ -393,32 +542,57 @@
     layer_scale,
     cotangent,
 ):
-    reach = kernel.shape[0] // 2
     shape = images.shape
-    channels = shape[3]
-    side_pad = ((0, 0), (0, 0), (reach, reach), (0, 0))
-    extended = extended_2(images, (("rows", 1),), reach)
-    padded = jnp.pad(extended.astype(jnp.float32), side_pad)
-    conv_out = depthwise(padded, kernel) + conv_bias
-    grad_conv, scaled, activated, normed, grad_before = block_terms(
-        conv_out.reshape(-1, channels),
-        norm_gain,
-        norm_shift,
+    channels, hidden = up_weight.shape
+    pixels = shape[0] * shape[1] * shape[2]
+    groups, parts = lax.axis_size("dp"), lax.axis_size("rows")
+    factor = 1.0 / math.sqrt(pixels * groups * parts)
+    scratch = reduce_scratch() | dict(
+        source=pltpu.VMEM((HROWS + 2 * REACH, COLS, channels), F32),
+        gradient=pltpu.VMEM((HROWS + 2 * REACH, COLS, channels), F32),
+        conv=pltpu.VMEM((HROWS, COLS, channels), F32),
+        scaled=pltpu.VMEM((pixels, channels), BF16),
+        spread_scaled=pltpu.VMEM((pixels, NY * 128), BF16),
+        grad_act=pltpu.VMEM((pixels, hidden), F32),
+        standard=pltpu.VMEM((pixels, channels), F32),
+        inverse=pltpu.VMEM((pixels, 1), F32),
+        normed=pltpu.VMEM((pixels, channels), BF16),
+        spread_normed=pltpu.VMEM((HALF, NY * 128), BF16),
+        before=pltpu.VMEM((HALF, NX * NC * HB), F32),
+        activated=pltpu.VMEM((HALF, NX * NC * HB), BF16),
+        slope=pltpu.VMEM((HALF, NX * NC * HB), BF16),
+        grad_normed=pltpu.VMEM((HALF, channels), F32),
+        grad_conv=pltpu.VMEM((pixels, channels), BF16),
+        image_halo=pltpu.VMEM((2, REACH * COLS, channels), BF16),
+        grad_halo=pltpu.VMEM((2, REACH * COLS, channels), BF16),
+        image_sems=pltpu.SemaphoreType.DMA((2, 2)),
+        grad_sems=pltpu.SemaphoreType.DMA((2, 2)),
+    )
+    block = jax.ShapeDtypeStruct((CB, HB), F32)
+    vmem = pl.BlockSpec(memory_space=pltpu.VMEM)
+    row = lambda vector: vector.reshape(1, -1)
+    grad_images, grad_up, grad_down = pl.pallas_call(
+        functools.partial(block_kernel, factor, tuple(scratch)),
+        out_shape=(jax.ShapeDtypeStruct((pixels, channels), BF16), block, block),
+        in_specs=[vmem] * 10,
+        out_specs=(vmem, vmem, vmem),
+        scratch_shapes=list(scratch.values()),
+        compiler_params=pltpu.CompilerParams(
+            collective_id=0, has_side_effects=True, vmem_limit_bytes=56 * 1024 * 1024
+        ),
+    )(
+        images.reshape(pixels, channels),
+        kernel,
+        row(conv_bias),
+        row(norm_gain),
+        row(norm_shift),
         up_weight,
-        up_bias,
+        row(up_bias),
         down_weight,
-        layer_scale,
-        cotangent.reshape(-1, channels),
+        row(layer_scale),
+        cotangent.reshape(pixels, channels),
     )
-    grad_ext = extended_2(grad_conv.reshape(shape), (("rows", 1),), reach)
-    grad_pad = jnp.pad(grad_ext.astype(jnp.float32), side_pad)
-    back = depthwise(grad_pad, kernel[::-1, ::-1])
-    grad_images = (cotangent.astype(jnp.float32) + back).astype(jnp.bfloat16)
-    groups = lax.axis_size("dp")
-    parts = lax.axis_size("rows")
-    factor = 1.0 / math.sqrt(shape[0] * shape[1] * shape[2] * groups * parts)
-    grad_up, grad_down = weight_sums(factor, scaled, activated, normed, grad_before)
-    return (grad_images, grad_up, grad_down)
+    return (grad_images.reshape(shape), grad_up, grad_down)
 
 
 def solution(mesh):

time: 167 us -> 103 us (0.62)
  the two profiles are of different devices: /device:TPU:4 before, /device:TPU:24 now
where the time goes in v2:
time: 103 us; the launch traced here: 102 us
  Pallas kernels  90.8 us (88%)
  local copies, waits for them, and re-layouts  10.7 us (10%)
    pallas_call x1, Pallas kernels, on_device(): pl.pallas_call(functools.partial(block_kernel, factor, tuple(scratch)), o...  90.8 us
    reshape x5, local copies, waits for them, and re-layouts, on_device(): row = lambda vector: vector.reshape(1, -1)  6.31 us
    unnamed x3, local copies, waits for them, and re-layouts  4.37 us

profile of v2, /device:TPU:24, one launch (start us, length us, event | category | flops | bytes accessed | tf_op | source)
XLA Modules:
  0.0 102.1 jit_solution(2427601014625866310)
XLA Ops:
  0.6 1.2 %reshape.31.conv_bias = f32[1,384]{1,0:T(1,128)} reshape(f32[384]{0:T(512)} %param.12) | data formatting | bytes 3072 | tf_op jit(solution)/shard_map/reshape | solution.py:573
  1.9 1.2 %reshape.32.gain = f32[1,384]{1,0:T(1,128)} reshape(f32[384]{0:T(512)} %param.13) | data formatting | bytes 3072 | tf_op jit(solution)/shard_map/reshape | solution.py:573
  3.1 1.3 %reshape.33.shift = f32[1,384]{1,0:T(1,128)} reshape(f32[384]{0:T(512)} %param.14) | data formatting | bytes 3072 | tf_op jit(solution)/shard_map/reshape | solution.py:573
  4.4 1.3 %reshape.35.scale = f32[1,384]{1,0:T(1,128)} reshape(f32[384]{0:T(512)} %param.18) | data formatting | bytes 3072 | tf_op jit(solution)/shard_map/reshape | solution.py:573
  5.6 1.3 %reshape.34.up_bias = f32[1,1536]{1,0:T(1,128)} reshape(f32[1536]{0:T(1024)} %param.16) | data formatting | bytes 12288 | tf_op jit(solution)/shard_map/reshape | solution.py:573
  6.9 90.8 %shard_map.121 = (bf16[512,384]{1,0:T(8,128)(2,1)}, f32[12,48]{1,0:T(8,128)}, f32[12,48]{1,0:T(8,128)}) custom-call(bf16[512,384]{1,0:T(8,128)(2,1)} %bitcast.3, f32[7,7,384]{2,1,0:T(8,128)} %kernel.1, f32[1,384]{1,0:T(1,128)} %reshape.31.conv_bias, f32[1,384]{1,0:T(1,128)} %reshape.32.gain, f32[1,384]{1,0:T(1,128)} %reshape.33.shift, ...), custom_call_target="tpu_custom_call" | custom-call | tf_op jit(solution)/shard_map/pallas_call | solution.py:574
  97.8 1.8 %copy.16 = bf16[1,8,64,384]{3,2,1,0:T(8,128)(2,1)} copy(bf16[1,8,64,384]{3,2,1,0:T(8,128)(2,1)} %bitcast.5) | data formatting | bytes 786432
  99.5 1.3 %copy.17 = f32[12,48]{1,0:T(8,128)} copy(f32[12,48]{1,0:T(8,128)} %get-tuple-element.13) | data formatting | bytes 4608
  100.8 1.3 %copy.18 = f32[12,48]{1,0:T(8,128)} copy(f32[12,48]{1,0:T(8,128)} %get-tuple-element.14) | data formatting | bytes 4608

commit v3 on v2

--- a/solution.py
+++ b/solution.py
@@ -150,12 +150,9 @@
         core = self.peers.at[2]
         value = lax.dot_general(left, right, (((0,), (0,)), ((), ())), preferred_element_type=F32)
 
-        @pl.when(jnp.logical_not(last))
-        def _():
+        if not last:
             self.total[g, z] = value
-
-        @pl.when(last)
-        def _():
+        else:
             whole = (value + self.total[g, z]).reshape(NX, NC, HB, NY * 128)
             self.own[g, z] = jnp.where(core == 0, whole[:, 0], whole[:, 1])
             self.b1[g, z] = jnp.where(core == 0, whole[:, 1], whole[:, 0]).astype(BF16)
@@ -309,7 +306,8 @@
 
 KS, REACH = 7, 3
 HROWS, COLS = 8, 64
-HALF = HROWS // 2 * COLS
+PARTS = (HROWS - REACH, REACH)
+MOST = PARTS[0] * COLS
 
 
 def row_sum(rows, kernel_ref, lanes, flip):
@@ -368,7 +366,7 @@
     return values * cdf, cdf + values * density
 
 
-def block_kernel(factor, names, images, kernel, conv_bias, gain, shift, up_weight, up_bias, down_weight, scale, cotangent,
+def block_kernel(factor, names, images, kernel, conv_bias, gain, shift, up_whole, up_bias, down_whole, scale, cotangent,
                  out, up_out, down_out, *scratch):
     s = dict(zip(names, scratch))
     peers = Peers()
@@ -377,6 +375,11 @@
     sums = Reduction(peers, s)
     zh, x, c, y, zl = peers.at
     strip = (zh * NX + x) * NC + c
+    up_weight, down_weight = s["up_weight"], s["down_weight"]
+    down_copy = pltpu.make_async_copy(down_whole, down_weight, s["weight_sems"].at[0])
+    up_copy = pltpu.make_async_copy(up_whole, up_weight, s["weight_sems"].at[1])
+    down_copy.start()
+    up_copy.start()
     channels, hidden = up_weight.shape
     width = NX * NC * HB
     source, gradient, conv = s["source"], s["gradient"], s["conv"]
@@ -384,6 +387,9 @@
     standard, inverse, normed, spread_normed = s["standard"], s["inverse"], s["normed"], s["spread_normed"]
     before, activated, slope, grad_normed, grad_conv = s["before"], s["activated"], s["slope"], s["grad_normed"], s["grad_conv"]
 
+    def row(vector):
+        return vector[...].reshape(1, channels)
+
     def chunk(n):
         return pl.ds(pl.multiple_of(n * width, 128), width)
 
@@ -406,85 +412,88 @@
     def _(h):
         at = pl.ds(pl.multiple_of(h * COLS, COLS), COLS)
         source[REACH + h] = images[at, :].astype(F32)
-        scaled[at, :] = (cotangent[at, :].astype(F32) * scale[...]).astype(BF16)
+        scaled[at, :] = (cotangent[at, :].astype(F32) * row(scale)).astype(BF16)
 
     own_rows(source, conv, kernel, False)
     spread_scaled[...] = spread_channels(scaled[...])
+
+    await_greetings(others)
+    for side in (0, 1):
+
+        @pl.when(has_neighbour(side))
+        def _(side=side):
+            halo_copy(images, s["image_halo"], s["image_sems"], side).start()
+
+    down_copy.wait()
 
     @pl.loop(0, NZH)
     def _(n):
         grad_act[:, chunk(n)] = jnp.dot(scaled[...], down_weight[:, chunk(n)], preferred_element_type=F32)
 
-    await_greetings(others)
-    for side in (0, 1):
+    up_copy.wait()
+    early = jnp.where((x == 0) & (c == 0), 1, 0)
+
+    def part(rows, first, side, last):
+        size = rows * COLS
 
         @pl.when(has_neighbour(side))
-        def _(side=side):
-            halo_copy(images, s["image_halo"], s["image_sems"], side).start()
-
-    early = jnp.where((x == 0) & (c == 0), 1, 0)
-
-    @pl.loop(0, 2)
-    def _(step):
-        half = jnp.where(step == 0, early, 1 - early)
-        last = step == 1
-
-        @pl.when(has_neighbour(half))
         def _():
-            arrived(images, s["image_halo"], s["image_sems"], half)
-            halo_rows(s["image_halo"], half, conv, kernel, False)
-
-        pixels = pl.ds(pl.multiple_of(half * HALF, HALF), HALF)
-
-        @pl.loop(0, HROWS // 2)
+            arrived(images, s["image_halo"], s["image_sems"], side)
+            halo_rows(s["image_halo"], side, conv, kernel, False)
+
+        pixels = pl.ds(pl.multiple_of(first * COLS, COLS), size)
+
+        @pl.loop(0, rows)
         def _(k):
-            h = half * (HROWS // 2) + k
+            h = first + k
             at = pl.ds(pl.multiple_of(h * COLS, COLS), COLS)
-            value = conv[h] + conv_bias[...]
+            value = conv[h] + row(conv_bias)
             centered = value - jnp.sum(value, axis=1, keepdims=True) * (1.0 / channels)
             inv = lax.rsqrt(jnp.sum(centered * centered, axis=1, keepdims=True) * (1.0 / channels) + EPSILON)
             std = centered * inv
             standard[at, :] = std
             inverse[at, :] = inv
-            normed[at, :] = (std * gain[...] + shift[...]).astype(BF16)
-
-        spread_normed[...] = spread_channels(normed[pixels, :])
+            normed[at, :] = (std * row(gain) + row(shift)).astype(BF16)
+
+        spread_normed[:size] = spread_channels(normed[pixels, :])
 
         @pl.loop(0, NZH)
         def _(n):
             weights = up_weight[:, chunk(n)]
-            before[...] = jnp.dot(normed[pixels, :], weights, preferred_element_type=F32)
-
-            @pl.loop(0, HALF // TILE)
+            before[:size] = jnp.dot(normed[pixels, :], weights, preferred_element_type=F32)
+
+            @pl.loop(0, size // TILE)
             def _(k):
                 at = pl.ds(pl.multiple_of(k * TILE, TILE), TILE)
-                act, slopes = gelu_parts(before[at, :] + up_bias[:, chunk(n)])
+                act, slopes = gelu_parts(before[at, :] + up_bias[chunk(n)].reshape(1, width))
                 activated[at, :] = act.astype(BF16)
-                grads = grad_act[pl.ds(pl.multiple_of(half * HALF + k * TILE, TILE), TILE), chunk(n)]
+                grads = grad_act[pl.ds(pl.multiple_of(first * COLS + k * TILE, TILE), TILE), chunk(n)]
                 slope[at, :] = (grads * slopes).astype(BF16)
 
-            sums.term(DOWN, n, activated[...], spread_scaled[pixels, :], last)
-            sums.term(UP, n, slope[...], spread_normed[...], last)
-            back = lax.dot_general(slope[...], weights, (((1,), (1,)), ((), ())), preferred_element_type=F32)
+            sums.term(DOWN, n, activated[:size], spread_scaled[pixels, :], last)
+            sums.term(UP, n, slope[:size], spread_normed[:size], last)
+            back = lax.dot_general(slope[:size], weights, (((1,), (1,)), ((), ())), preferred_element_type=F32)
 
             @pl.when(n == 0)
             def _():
-                grad_normed[...] = back
+                grad_normed[:size] = back
 
             @pl.when(n > 0)
             def _():
-                grad_normed[...] = grad_normed[...] + back
-
-            @pl.when(last & (n > 0))
-            def _():
-                sums.second(DOWN, n - 1)
-                sums.second(UP, n - 1)
-
-        @pl.loop(0, HROWS // 2)
+                grad_normed[:size] = grad_normed[:size] + back
+
+            if last:
+
+                @pl.when(n > 0)
+                def _():
+                    sums.second(DOWN, n - 1)
+                    sums.second(UP, n - 1)
+
+        @pl.loop(0, rows)
         def _(k):
-            h = half * (HROWS // 2) + k
+            h = first + k
             at = pl.ds(pl.multiple_of(h * COLS, COLS), COLS)
-            gscaled = grad_normed[pl.ds(pl.multiple_of(k * COLS, COLS), COLS), :] * gain[...]
+            gscaled = grad_normed[pl.ds(pl.multiple_of(k * COLS, COLS), COLS), :] * row(gain)
             std = standard[at, :]
             mean = jnp.sum(gscaled, axis=1, keepdims=True) * (1.0 / channels)
             along = jnp.sum(gscaled * std, axis=1, keepdims=True) * (1.0 / channels)
@@ -492,10 +501,12 @@
             grad_conv[at, :] = value
             gradient[REACH + h] = value.astype(F32)
 
-        @pl.when(has_neighbour(half))
+        @pl.when(has_neighbour(side))
         def _():
-            halo_copy(grad_conv, s["grad_halo"], s["grad_sems"], half).start()
-
+            halo_copy(grad_conv, s["grad_halo"], s["grad_sems"], side).start()
+
+    part(PARTS[0], early * REACH, early, False)
+    part(PARTS[1], (1 - early) * PARTS[0], 1 - early, True)
     for g in (DOWN, UP):
         sums.second(g, NZH - 1)
     own_rows(gradient, conv, kernel, True)
@@ -528,6 +539,12 @@
 
 
 TILE = 64
+
+
+def hand_over(images, up, down, images_out, up_out, down_out):
+    images_out[...] = images[...]
+    up_out[...] = up[...]
+    down_out[...] = down[...]
 
 
 def on_device(
@@ -551,17 +568,20 @@
         source=pltpu.VMEM((HROWS + 2 * REACH, COLS, channels), F32),
         gradient=pltpu.VMEM((HROWS + 2 * REACH, COLS, channels), F32),
         conv=pltpu.VMEM((HROWS, COLS, channels), F32),
+        up_weight=pltpu.VMEM(up_weight.shape, BF16),
+        down_weight=pltpu.VMEM(down_weight.shape, BF16),
+        weight_sems=pltpu.SemaphoreType.DMA((2,)),
         scaled=pltpu.VMEM((pixels, channels), BF16),
         spread_scaled=pltpu.VMEM((pixels, NY * 128), BF16),
         grad_act=pltpu.VMEM((pixels, hidden), F32),
         standard=pltpu.VMEM((pixels, channels), F32),
         inverse=pltpu.VMEM((pixels, 1), F32),
         normed=pltpu.VMEM((pixels, channels), BF16),
-        spread_normed=pltpu.VMEM((HALF, NY * 128), BF16),
-        before=pltpu.VMEM((HALF, NX * NC * HB), F32),
-        activated=pltpu.VMEM((HALF, NX * NC * HB), BF16),
-        slope=pltpu.VMEM((HALF, NX * NC * HB), BF16),
-        grad_normed=pltpu.VMEM((HALF, channels), F32),
+        spread_normed=pltpu.VMEM((MOST, NY * 128), BF16),
+        before=pltpu.VMEM((MOST, NX * NC * HB), F32),
+        activated=pltpu.VMEM((MOST, NX * NC * HB), BF16),
+        slope=pltpu.VMEM((MOST, NX * NC * HB), BF16),
+        grad_normed=pltpu.VMEM((MOST, channels), F32),
         grad_conv=pltpu.VMEM((pixels, channels), BF16),
         image_halo=pltpu.VMEM((2, REACH * COLS, channels), BF16),
         grad_halo=pltpu.VMEM((2, REACH * COLS, channels), BF16),
@@ -569,12 +589,11 @@
         grad_sems=pltpu.SemaphoreType.DMA((2, 2)),
     )
     block = jax.ShapeDtypeStruct((CB, HB), F32)
-    vmem = pl.BlockSpec(memory_space=pltpu.VMEM)
-    row = lambda vector: vector.reshape(1, -1)
+    vmem, anywhere = pl.BlockSpec(memory_space=pltpu.VMEM), pl.BlockSpec(memory_space=pl.ANY)
     grad_images, grad_up, grad_down = pl.pallas_call(
         functools.partial(block_kernel, factor, tuple(scratch)),
         out_shape=(jax.ShapeDtypeStruct((pixels, channels), BF16), block, block),
-        in_specs=[vmem] * 10,
+        in_specs=[vmem] * 5 + [anywhere, vmem, anywhere, vmem, vmem],
         out_specs=(vmem, vmem, vmem),
         scratch_shapes=list(scratch.values()),
         compiler_params=pltpu.CompilerParams(
@@ -583,15 +602,21 @@
     )(
         images.reshape(pixels, channels),
         kernel,
-        row(conv_bias),
-        row(norm_gain),
-        row(norm_shift),
+        conv_bias,
+        norm_gain,
+        norm_shift,
         up_weight,
-        row(up_bias),
+        up_bias,
         down_weight,
-        row(layer_scale),
+        layer_scale,
         cotangent.reshape(pixels, channels),
     )
+    grad_images, grad_up, grad_down = pl.pallas_call(
+        hand_over,
+        out_shape=(jax.ShapeDtypeStruct((pixels, channels), BF16), block, block),
+        in_specs=[vmem] * 3,
+        out_specs=(vmem, vmem, vmem),
+    )(grad_images, grad_up, grad_down)
     return (grad_images.reshape(shape), grad_up, grad_down)
 
 

time: 103 us -> 91.1 us (0.88)
  local copies, waits for them, and re-layouts: 10.7 us -> 0 us
    reshape x5 -> x0, local copies, waits for them, and re-layouts: 6.31 us -> none  [on_device(): row = lambda vector: vector.reshape(1, -1)]
    unnamed x3 -> x0, local copies, waits for them, and re-layouts: 4.37 us -> none
    pallas_call x1, Pallas kernels: 90.8 us -> 88.4 us  [on_device(): pl.pallas_call(functools.partial(block_kernel, factor, tuple(scratch)), o...]
    pallas_call x0 -> x1, Pallas kernels: none -> 1.8 us  [on_device(): pl.pallas_call(hand_over, out_shape=(jax.ShapeDtypeStruct((pixels, channe...]
where the time goes in v3:
time: 91.1 us; the launch traced here: 90.9 us
  Pallas kernels  90.2 us (99%)
    pallas_call x1, Pallas kernels, on_device(): pl.pallas_call(functools.partial(block_kernel, factor, tuple(scratch)), o...  88.4 us

profile of v3, /device:TPU:24, one launch (start us, length us, event | category | flops | bytes accessed | tf_op | source)
XLA Modules:
  0.0 90.9 jit_solution(9951317687730461514)
XLA Ops:
  0.6 88.4 %shard_map.121 = (bf16[512,384]{1,0:T(8,128)(2,1)}, f32[12,48]{1,0:T(8,128)}, f32[12,48]{1,0:T(8,128)}) custom-call(bf16[512,384]{1,0:T(8,128)(2,1)} %bitcast.3, f32[7,7,384]{2,1,0:T(8,128)} %kernel.1, f32[384]{0:T(512)} %conv_bias.1, f32[384]{0:T(512)} %gain.1, f32[384]{0:T(512)} %shift.1, bf16[384,1536]{1,0:T(8,128)(2,1)} %up_whole.1, f32[1536]{0:T(1024)} %up_bias.1, ...), custom_call_target="tpu_custom_call" | custom-call | tf_op jit(solution)/shard_map/pallas_call | solution.py:593
  89.1 1.8 %shard_map.122 = (bf16[512,384]{1,0:T(8,128)(2,1)}, f32[12,48]{1,0:T(8,128)}, f32[12,48]{1,0:T(8,128)}) custom-call(bf16[512,384]{1,0:T(8,128)(2,1)} %get-tuple-element.9.images, f32[12,48]{1,0:T(8,128)} %get-tuple-element.10.up, f32[12,48]{1,0:T(8,128)} %get-tuple-element.11.down), custom_call_target="tpu_custom_call" | custom-call | tf_op jit(solution)/shard_map/pallas_call | solution.py:614

commit v4 on v3

--- a/solution.py
+++ b/solution.py
@@ -366,8 +366,8 @@
     return values * cdf, cdf + values * density
 
 
-def block_kernel(factor, names, images, kernel, conv_bias, gain, shift, up_whole, up_bias, down_whole, scale, cotangent,
-                 out, up_out, down_out, *scratch):
+def block_kernel(factor, names, images_whole, kernel, conv_bias, gain, shift, up_whole, up_bias, down_whole, scale,
+                 cotangent_whole, out_whole, up_out, down_out, *scratch):
     s = dict(zip(names, scratch))
     peers = Peers()
     others = peers.all()
@@ -375,11 +375,14 @@
     sums = Reduction(peers, s)
     zh, x, c, y, zl = peers.at
     strip = (zh * NX + x) * NC + c
-    up_weight, down_weight = s["up_weight"], s["down_weight"]
-    down_copy = pltpu.make_async_copy(down_whole, down_weight, s["weight_sems"].at[0])
-    up_copy = pltpu.make_async_copy(up_whole, up_weight, s["weight_sems"].at[1])
-    down_copy.start()
-    up_copy.start()
+    images, cotangent, up_weight, down_weight, out = (
+        s[name] for name in ("images", "cotangent", "up_weight", "down_weight", "out")
+    )
+    loads = ((images_whole, images), (cotangent_whole, cotangent), (down_whole, down_weight), (up_whole, up_weight))
+    loads = [pltpu.make_async_copy(*pair, s["load_sems"].at[k]) for k, pair in enumerate(loads)]
+    store = pltpu.make_async_copy(out, out_whole, s["load_sems"].at[len(loads)])
+    for load in loads:
+        load.start()
     channels, hidden = up_weight.shape
     width = NX * NC * HB
     source, gradient, conv = s["source"], s["gradient"], s["conv"]
@@ -408,6 +411,9 @@
         rows[:REACH] = jnp.zeros((REACH, COLS, channels), F32)
         rows[REACH + HROWS :] = jnp.zeros((REACH, COLS, channels), F32)
 
+    loads[0].wait()
+    loads[1].wait()
+
     @pl.loop(0, HROWS)
     def _(h):
         at = pl.ds(pl.multiple_of(h * COLS, COLS), COLS)
@@ -415,8 +421,6 @@
         scaled[at, :] = (cotangent[at, :].astype(F32) * row(scale)).astype(BF16)
 
     own_rows(source, conv, kernel, False)
-    spread_scaled[...] = spread_channels(scaled[...])
-
     await_greetings(others)
     for side in (0, 1):
 
@@ -424,13 +428,14 @@
         def _(side=side):
             halo_copy(images, s["image_halo"], s["image_sems"], side).start()
 
-    down_copy.wait()
+    spread_scaled[...] = spread_channels(scaled[...])
+    loads[2].wait()
 
     @pl.loop(0, NZH)
     def _(n):
         grad_act[:, chunk(n)] = jnp.dot(scaled[...], down_weight[:, chunk(n)], preferred_element_type=F32)
 
-    up_copy.wait()
+    loads[3].wait()
     early = jnp.where((x == 0) & (c == 0), 1, 0)
 
     def part(rows, first, side, last):
@@ -513,6 +518,7 @@
     for g in (DOWN, UP):
         sums.third(g)
     sums.fourth()
+    sums.fifth()
     for step in (0, 1):
         side = jnp.where(step == 0, early, 1 - early)
 
@@ -526,10 +532,11 @@
         at = pl.ds(pl.multiple_of(h * COLS, COLS), COLS)
         out[at, :] = (cotangent[at, :].astype(F32) + conv[h]).astype(BF16)
 
-    sums.fifth()
+    store.start()
     sums.sixth()
     sums.finish(factor, up_out, down_out)
     sums.drain()
+    store.wait()
     for strip_ref, halo, sems in ((images, s["image_halo"], s["image_sems"]), (grad_conv, s["grad_halo"], s["grad_sems"])):
         for side in (0, 1):
 
@@ -541,10 +548,12 @@
 TILE = 64
 
 
-def hand_over(images, up, down, images_out, up_out, down_out):
-    images_out[...] = images[...]
+def hand_over(images, up, down, images_out, up_out, down_out, sem):
+    copy = pltpu.make_async_copy(images, images_out, sem)
+    copy.start()
     up_out[...] = up[...]
     down_out[...] = down[...]
+    copy.wait()
 
 
 def on_device(
@@ -570,7 +579,10 @@
         conv=pltpu.VMEM((HROWS, COLS, channels), F32),
         up_weight=pltpu.VMEM(up_weight.shape, BF16),
         down_weight=pltpu.VMEM(down_weight.shape, BF16),
-        weight_sems=pltpu.SemaphoreType.DMA((2,)),
+        images=pltpu.VMEM((pixels, channels), BF16),
+        cotangent=pltpu.VMEM((pixels, channels), BF16),
+        out=pltpu.VMEM((pixels, channels), BF16),
+        load_sems=pltpu.SemaphoreType.DMA((5,)),
         scaled=pltpu.VMEM((pixels, channels), BF16),
         spread_scaled=pltpu.VMEM((pixels, NY * 128), BF16),
         grad_act=pltpu.VMEM((pixels, hidden), F32),
@@ -593,8 +605,8 @@
     grad_images, grad_up, grad_down = pl.pallas_call(
         functools.partial(block_kernel, factor, tuple(scratch)),
         out_shape=(jax.ShapeDtypeStruct((pixels, channels), BF16), block, block),
-        in_specs=[vmem] * 5 + [anywhere, vmem, anywhere, vmem, vmem],
-        out_specs=(vmem, vmem, vmem),
+        in_specs=[anywhere] + [vmem] * 4 + [anywhere, vmem, anywhere, vmem, anywhere],
+        out_specs=(anywhere, vmem, vmem),
         scratch_shapes=list(scratch.values()),
         compiler_params=pltpu.CompilerParams(
             collective_id=0, has_side_effects=True, vmem_limit_bytes=56 * 1024 * 1024
@@ -614,8 +626,9 @@
     grad_images, grad_up, grad_down = pl.pallas_call(
         hand_over,
         out_shape=(jax.ShapeDtypeStruct((pixels, channels), BF16), block, block),
-        in_specs=[vmem] * 3,
-        out_specs=(vmem, vmem, vmem),
+        in_specs=[anywhere, vmem, vmem],
+        out_specs=(anywhere, vmem, vmem),
+        scratch_shapes=[pltpu.SemaphoreType.DMA],
     )(grad_images, grad_up, grad_down)
     return (grad_images.reshape(shape), grad_up, grad_down)
 

time: 91.1 us -> 103 us (1.13)
  Pallas kernels: 90.2 us -> 102 us
    pallas_call x1, Pallas kernels: 1.8 us -> 14.3 us  [on_device(): pl.pallas_call(hand_over, out_shape=(jax.ShapeDtypeStruct((pixels, channe...]
where the time goes in v4:
time: 103 us
  Pallas kernels  102 us (99%)
    pallas_call x1, Pallas kernels, on_device(): pl.pallas_call(functools.partial(block_kernel, factor, tuple(scratch)), o...  87.9 us
    pallas_call x1, Pallas kernels, on_device(): pl.pallas_call(hand_over, out_shape=(jax.ShapeDtypeStruct((pixels, channe...  14.3 us

profile of v4, /device:TPU:24, one launch (start us, length us, event | category | flops | bytes accessed | tf_op | source)
XLA Modules:
  0.0 102.9 jit_solution(1132162601650153672)
XLA Ops:
  0.6 87.9 %shard_map.121 = (bf16[512,384]{1,0:T(8,128)(2,1)}, f32[12,48]{1,0:T(8,128)}, f32[12,48]{1,0:T(8,128)}) custom-call(bf16[512,384]{1,0:T(8,128)(2,1)} %bitcast.3, f32[7,7,384]{2,1,0:T(8,128)} %kernel.1, f32[384]{0:T(512)} %conv_bias.1, f32[384]{0:T(512)} %gain.1, f32[384]{0:T(512)} %shift.1, bf16[384,1536]{1,0:T(8,128)(2,1)} %up_whole.1, f32[1536]{0:T(1024)} %up_bias.1, ...), custom_call_target="tpu_custom_call" | custom-call | tf_op jit(solution)/shard_map/pallas_call | solution.py:605
  88.6 14.3 %shard_map.122 = (bf16[512,384]{1,0:T(8,128)(2,1)}, f32[12,48]{1,0:T(8,128)}, f32[12,48]{1,0:T(8,128)}) custom-call(bf16[512,384]{1,0:T(8,128)(2,1)} %get-tuple-element.9.images, f32[12,48]{1,0:T(8,128)} %get-tuple-element.10.up, f32[12,48]{1,0:T(8,128)} %get-tuple-element.11.down), custom_call_target="tpu_custom_call" | custom-call | tf_op jit(solution)/shard_map/pallas_call | solution.py:626
